TPU v7x, 32 devices: a whole 2x2x4 slice. The times are simulated.
32 devices in a mesh: bucket: 4 (over y, x), head: 8 (over z, core).
Axes of the slice: x: 2, y: 2, z: 4, core: 2. Of those that a mesh axis runs over, the one named last changes fastest.
Arguments:
- queries: bfloat16 [4096, 4096], P(('bucket', 'head')), may hold values from -25 to 25
- keys: bfloat16 [4096, 4096], P(('bucket', 'head')), may hold values from -6 to 6
- values: bfloat16 [4096, 4096], P(('bucket', 'head')), may hold values from -6 to 6
- grad_out: bfloat16 [4096, 4096], P(('bucket', 'head')), may hold values from -6 to 6
- page_dest: int32 [128], replicated, may hold values from 0 to 127, as said below
- doc_start: int32 [128], replicated, may hold values from 0 to 24, as said below
Outputs:
- grad_queries: bfloat16 [4096, 4096], P(('bucket', 'head'))
- grad_keys: bfloat16 [4096, 4096], P(('bucket', 'head'))
- grad_values: bfloat16 [4096, 4096], P(('bucket', 'head'))
Inputs may be any that keep to these rules, and one draw needn't show every extreme that they name: Page p holds window tokens p * 32 to p * 32 + 31. page_dest[p] = bucket * 32 + slot; the 4 pages of each device go one to each bucket, and every slot of every bucket is named by exactly one page. doc_start[bucket * 32 + slot] is the first slot of the document that holds that slot. Documents are runs of slots of one bucket, of lengths that are multiples of 8 slots, from 8 to 32; some bucket holds one document and some bucket ends with a document of the least length.
All inputs are finite; a program needn't handle non-finite values.
Results may differ from a plain program's by a relative error of at most 0.0081.
Values may be sent and summed in bfloat16 or wider, within the bound.
A program may use at most 128 MiB of HBM per device.

v0:
```python
import jax
import jax.numpy as jnp
from jax import lax
from jax.sharding import PartitionSpec as P

HD = 128


def routing(page_dest, doc_start, bucket_index, n_bucket, n_head, page_len):
    slot_count = n_bucket * n_head
    dest_table = page_dest.reshape(n_bucket, n_head, n_bucket)
    dest_bucket = dest_table // slot_count
    arriving = (dest_bucket == bucket_index).astype(jnp.int32)
    source_slot = jnp.sum(arriving * (dest_table % slot_count), axis=2)
    arrival_slot = jnp.transpose(source_slot).reshape(slot_count)
    slot_range = jnp.arange(slot_count, dtype=jnp.int32)
    matches = (arrival_slot[:, None] == slot_range[None, :]).astype(jnp.int32)
    slot_order = jnp.sum(matches * slot_range[:, None], axis=0)
    doc_slots = lax.dynamic_slice_in_dim(doc_start, bucket_index * slot_count, slot_count)
    token_start = jnp.repeat(doc_slots * page_len, page_len)
    return (dest_bucket, arrival_slot, slot_order, token_start)


def group_segment(array_in, page_pick, n_head, n_bucket, page_len, columns):
    shaped = array_in.reshape(n_head, n_bucket, page_len, columns)
    return jnp.take_along_axis(shaped, page_pick[:, :, None, None], axis=1)


def to_slots(array_in, slot_order, pages_all, page_len, columns, heads_local):
    shaped = array_in.reshape(pages_all, page_len, columns)
    return jnp.take(shaped, slot_order, axis=0).reshape(pages_all * page_len, heads_local, HD)


def from_slots(array_in, arrival_slot, n_head, n_bucket, page_len, columns):
    shaped = array_in.reshape(n_head * n_bucket, page_len, columns)
    return jnp.take(shaped, arrival_slot, axis=0).reshape(n_head, n_bucket, page_len, columns)


def attention_grads(query_all, key_all, value_all, cotan_all, token_start):
    seg_len, heads_local, head_dim = query_all.shape
    block_rows = min(512, seg_len)
    blocks = seg_len // block_rows
    score_scale = float(HD) ** (-0.5)
    key_pos = jnp.arange(seg_len, dtype=jnp.int32)

    def one_block(totals, block_index):
        grad_key, grad_value = totals
        row_first = block_index * block_rows
        query_blk = lax.dynamic_slice_in_dim(query_all, row_first, block_rows, 0)
        cotan_blk = lax.dynamic_slice_in_dim(cotan_all, row_first, block_rows, 0)
        start_blk = lax.dynamic_slice_in_dim(token_start, row_first, block_rows, 0)
        query_pos = row_first + jnp.arange(block_rows, dtype=jnp.int32)
        visible = (key_pos[None, :] <= query_pos[:, None]) & (
            key_pos[None, :] >= start_blk[:, None]
        )
        scores = (
            jnp.einsum("qhd,khd->hqk", query_blk, key_all, preferred_element_type=jnp.float32)
            * score_scale
        )
        scores = jnp.where(visible[None], scores, -jnp.inf)
        row_top = jnp.max(scores, axis=2, keepdims=True)
        weights = jnp.exp(scores - row_top)
        prob_low = (weights / jnp.sum(weights, axis=2, keepdims=True)).astype(jnp.bfloat16)
        attended = jnp.einsum(
            "hqk,khd->qhd", prob_low, value_all, preferred_element_type=jnp.float32
        ).astype(jnp.bfloat16)
        attended = lax.optimization_barrier(attended)
        row_dot = jnp.einsum(
            "qhd,qhd->hq", cotan_blk.astype(jnp.float32), attended.astype(jnp.float32)
        )
        grad_value = grad_value + jnp.einsum(
            "hqk,qhd->khd", prob_low, cotan_blk, preferred_element_type=jnp.float32
        )
        grad_prob = jnp.einsum(
            "qhd,khd->hqk", cotan_blk, value_all, preferred_element_type=jnp.float32
        )
        prob_kept = lax.optimization_barrier(prob_low)
        grad_score = (
            prob_kept.astype(jnp.float32) * (grad_prob - row_dot[:, :, None]) * score_scale
        ).astype(jnp.bfloat16)
        grad_query = jnp.einsum(
            "hqk,khd->qhd", grad_score, key_all, preferred_element_type=jnp.float32
        ).astype(jnp.bfloat16)
        grad_key = grad_key + jnp.einsum(
            "hqk,qhd->khd", grad_score, query_blk, preferred_element_type=jnp.float32
        )
        return ((grad_key, grad_value), grad_query)

    zeros_acc = jnp.zeros((seg_len, heads_local, head_dim), jnp.float32)
    (grad_key, grad_value), grad_query = lax.scan(
        one_block, (zeros_acc, zeros_acc), jnp.arange(blocks, dtype=jnp.int32)
    )
    columns = heads_local * head_dim
    return (
        grad_query.reshape(seg_len, columns),
        grad_key.astype(jnp.bfloat16).reshape(seg_len, columns),
        grad_value.astype(jnp.bfloat16).reshape(seg_len, columns),
    )


def shards(queries, keys, values, grad_out, page_dest, doc_start):
    n_bucket = lax.axis_size("bucket")
    n_head = lax.axis_size("head")
    bucket_index = lax.axis_index("bucket")
    tok_dev, width = queries.shape
    page_len = tok_dev // n_bucket
    columns = width // n_head
    heads_local = columns // HD
    pages_all = n_head * n_bucket
    dest_bucket, arrival_slot, slot_order, token_start = routing(
        page_dest, doc_start, bucket_index, n_bucket, n_head, page_len
    )
    page_range = jnp.arange(n_bucket, dtype=jnp.int32)
    seg_dest = lax.dynamic_index_in_dim(dest_bucket, bucket_index, 0, keepdims=False)
    page_pick = jnp.sum(
        (seg_dest[:, :, None] == page_range[None, None, :]).astype(jnp.int32)
        * page_range[None, :, None],
        axis=1,
    )
    narrow_q, narrow_k, narrow_v, narrow_g = (
        lax.all_to_all(queries, "head", split_axis=1, concat_axis=0, tiled=True),
        lax.all_to_all(keys, "head", split_axis=1, concat_axis=0, tiled=True),
        lax.all_to_all(values, "head", split_axis=1, concat_axis=0, tiled=True),
        lax.all_to_all(grad_out, "head", split_axis=1, concat_axis=0, tiled=True),
    )
    arrived = (
        lax.all_to_all(
            group_segment(narrow_q, page_pick, n_head, n_bucket, page_len, columns),
            "bucket",
            split_axis=1,
            concat_axis=1,
            tiled=True,
        ),
        lax.all_to_all(
            group_segment(narrow_k, page_pick, n_head, n_bucket, page_len, columns),
            "bucket",
            split_axis=1,
            concat_axis=1,
            tiled=True,
        ),
        lax.all_to_all(
            group_segment(narrow_v, page_pick, n_head, n_bucket, page_len, columns),
            "bucket",
            split_axis=1,
            concat_axis=1,
            tiled=True,
        ),
        lax.all_to_all(
            group_segment(narrow_g, page_pick, n_head, n_bucket, page_len, columns),
            "bucket",
            split_axis=1,
            concat_axis=1,
            tiled=True,
        ),
    )
    query_all = to_slots(arrived[0], slot_order, pages_all, page_len, columns, heads_local)
    key_all = to_slots(arrived[1], slot_order, pages_all, page_len, columns, heads_local)
    value_all = to_slots(arrived[2], slot_order, pages_all, page_len, columns, heads_local)
    cotan_all = to_slots(arrived[3], slot_order, pages_all, page_len, columns, heads_local)
    grad_query, grad_key, grad_value = attention_grads(
        query_all, key_all, value_all, cotan_all, token_start
    )
    back_q = from_slots(grad_query, arrival_slot, n_head, n_bucket, page_len, columns)
    back_k = from_slots(grad_key, arrival_slot, n_head, n_bucket, page_len, columns)
    back_v = from_slots(grad_value, arrival_slot, n_head, n_bucket, page_len, columns)
    home_q, home_k, home_v = (
        lax.all_to_all(back_q, "bucket", split_axis=1, concat_axis=1, tiled=True),
        lax.all_to_all(back_k, "bucket", split_axis=1, concat_axis=1, tiled=True),
        lax.all_to_all(back_v, "bucket", split_axis=1, concat_axis=1, tiled=True),
    )
    seg_len = n_head * tok_dev
    out_q, out_k, out_v = (
        lax.all_to_all(
            jnp.take_along_axis(home_q, seg_dest[:, :, None, None], axis=1).reshape(
                seg_len, columns
            ),
            "head",
            split_axis=0,
            concat_axis=1,
            tiled=True,
        ),
        lax.all_to_all(
            jnp.take_along_axis(home_k, seg_dest[:, :, None, None], axis=1).reshape(
                seg_len, columns
            ),
            "head",
            split_axis=0,
            concat_axis=1,
            tiled=True,
        ),
        lax.all_to_all(
            jnp.take_along_axis(home_v, seg_dest[:, :, None, None], axis=1).reshape(
                seg_len, columns
            ),
            "head",
            split_axis=0,
            concat_axis=1,
            tiled=True,
        ),
    )
    return (out_q, out_k, out_v)


def solution(mesh):
    in_specs = (
        P(("bucket", "head"), None),
        P(("bucket", "head"), None),
        P(("bucket", "head"), None),
        P(("bucket", "head"), None),
        P(),
        P(),
    )
    out_specs = (
        P(("bucket", "head"), None),
        P(("bucket", "head"), None),
        P(("bucket", "head"), None),
    )
    return jax.shard_map(shards, mesh=mesh, in_specs=in_specs, out_specs=out_specs, check_vma=False)
```

profile of v0, /device:TPU:0, one launch (start us, length us, event | category | flops | bytes accessed | tf_op | source)
XLA Modules:
  0.0 439.7 jit_solution(18415265804411179663)
XLA Ops:
  3.0 6.3 %all-to-all-start = ((bf16[128,8,512]{2,0,1:T(8,128)(2,1)}), bf16[128,8,512]{2,0,1:T(8,128)(2,1)S(1)}, u32[]{:S(2)}, u32[]{:S(2)}) async-start(bf16[128,8,512]{2,0,1:T(8,128)(2,1)} %bitcast.113), calls=%async_computation | async-start | bytes 2097152 | tf_op jit(solution)/shard_map/all_to_all | solution.py:121
  10.4 25.5 %all-to-all-done = bf16[128,8,512]{2,0,1:T(8,128)(2,1)S(1)} async-done(((bf16[128,8,512]{2,0,1:T(8,128)(2,1)}), bf16[128,8,512]{2,0,1:T(8,128)(2,1)S(1)}, u32[]{:S(2)}, u32[]{:S(2)}) %all-to-all-start) | async-done | bytes 1048608 | tf_op jit(solution)/shard_map/all_to_all | solution.py:121
  35.9 3.6 all-to-all-start.2
  41.8 24.2 %all-to-all-done.2 = bf16[128,8,512]{2,0,1:T(8,128)(2,1)S(1)} async-done(((bf16[128,8,512]{2,0,1:T(8,128)(2,1)}), bf16[128,8,512]{2,0,1:T(8,128)(2,1)S(1)}, u32[]{:S(2)}, u32[]{:S(2)}) %all-to-all-start.2) | async-done | bytes 1048608 | tf_op jit(solution)/shard_map/all_to_all | solution.py:122
  66.0 3.6 all-to-all-start.4
  71.9 24.2 %all-to-all-done.4 = bf16[128,8,512]{2,0,1:T(8,128)(2,1)S(1)} async-done(((bf16[128,8,512]{2,0,1:T(8,128)(2,1)}), bf16[128,8,512]{2,0,1:T(8,128)(2,1)S(1)}, u32[]{:S(2)}, u32[]{:S(2)}) %all-to-all-start.4) | async-done | bytes 1048608 | tf_op jit(solution)/shard_map/all_to_all | solution.py:124
  96.1 4.2 all-to-all-start.6
  104.1 22.9 %all-to-all-done.6 = bf16[128,8,512]{2,0,1:T(8,128)(2,1)} async-done(((bf16[128,8,512]{2,0,1:T(8,128)(2,1)}), bf16[128,8,512]{2,0,1:T(8,128)(2,1)}, u32[]{:S(2)}, u32[]{:S(2)}) %all-to-all-start.6) | async-done | bytes 1048608 | tf_op jit(solution)/shard_map/all_to_all | solution.py:123
  132.8 17.6 %all_to_all.156 = bf16[8,4,32,512]{3,2,0,1:T(8,128)(2,1)S(1)} all-to-all(bf16[8,4,32,512]{3,2,0,1:T(8,128)(2,1)S(1)} %get-tuple-element.200), channel_id=1, replica_groups=mesh['bucket'=4,'head'=8] {'bucket'}, dimensions={1} | all-to-all | bytes 2097152 | tf_op jit(solution)/shard_map/all_to_all | solution.py:127
  150.4 15.8 %all_to_all.157 = bf16[8,4,32,512]{3,2,0,1:T(8,128)(2,1)} all-to-all(bf16[8,4,32,512]{3,2,0,1:T(8,128)(2,1)S(1)} %get-tuple-element.198), channel_id=1, replica_groups=mesh['bucket'=4,'head'=8] {'bucket'}, dimensions={1} | all-to-all | bytes 2097152 | tf_op jit(solution)/shard_map/all_to_all | solution.py:134
  166.2 3.5 all-to-all-start.5
  170.0 10.6 %all-to-all-done.5 = bf16[8,4,32,512]{3,2,0,1:T(8,128)(2,1)S(1)} async-done(((bf16[8,4,32,512]{3,2,0,1:T(8,128)(2,1)}), bf16[8,4,32,512]{3,2,0,1:T(8,128)(2,1)S(1)}, u32[]{:S(2)}, u32[]{:S(2)}) %all-to-all-start.5) | async-done | bytes 1048608 | tf_op jit(solution)/shard_map/all_to_all | solution.py:148
  180.6 4.2 all-to-all-start.7
  203.4 4.0 broadcast_select_fusion.3
  219.9 61.1 %while.16 = (s32[]{:T(128)}, f32[1024,4,128]{0,2,1:T(8,128)S(1)}, f32[1024,4,128]{0,2,1:T(8,128)}, bf16[2,512,4,128]{3,2,1,0:T(4,128)(2,1)}, s32[2]{0:T(128)S(1)...) while((s32[]{:T(128)}, f32[1024,4,128]{0,2,1:T(8,128)S(1)}, ...), condition=%wide.region_6.9_spmd.clone.clone, body=%wide.region_3.8_spmd.clone.clone.sunk | while | flops 3249536512 | bytes 134261184 | solution.py:90
  224.2 7.6 %fusion.73 = (f32[4,512]{1,0:T(4,128)S(1)}, f32[4,512,1024]{2,1,0:T(8,128)}) fusion(pred[512,1024]{1,0:T(8,128)(4,1)} %fusion.72, bf16[1024,4,128]{2,0,1:T(8,128)(2,1)} %get-tuple-element.305, bf16[512,4,128]{2,1,0:T(4,128)(2,1)S(1)} %get-tuple-element.266), kind=kOutput, calls=%fused_computation.95.clone.1 | convolution fusion | flops 545260544 | bytes 10493952 | tf_op jit(solution)/shard_map/while/body/eval_jaxpr/sub | solution.py:62
  231.7 4.1 divide_convert_fusion.2
  240.8 3.5 bitcast_add_fusion.4
  253.9 7.5 %fusion.73 = (f32[4,512]{1,0:T(4,128)S(1)}, f32[4,512,1024]{2,1,0:T(8,128)}) fusion(pred[512,1024]{1,0:T(8,128)(4,1)} %fusion.72, bf16[1024,4,128]{2,0,1:T(8,128)(2,1)} %get-tuple-element.305, bf16[512,4,128]{2,1,0:T(4,128)(2,1)S(1)} %get-tuple-element.266), kind=kOutput, calls=%fused_computation.95.clone.1 | convolution fusion | flops 545260544 | bytes 10493952 | tf_op jit(solution)/shard_map/while/body/eval_jaxpr/sub | solution.py:62
  261.5 4.1 divide_convert_fusion.2
  270.6 3.5 bitcast_add_fusion.4
  277.0 3.9 bitcast_add_fusion.5
  295.0 4.1 all-to-all-start.10
  300.2 11.1 %all-to-all-done.10 = bf16[8,4,32,512]{3,2,0,1:T(8,128)(2,1)S(1)} async-done(((bf16[8,4,32,512]{3,2,0,1:T(8,128)(2,1)}), bf16[8,4,32,512]{3,2,0,1:T(8,128)(2,1)S(1)}, u32[]{:S(2)}, u32[]{:S(2)}) %all-to-all-start.10) | async-done | bytes 1048608 | tf_op jit(solution)/shard_map/all_to_all | solution.py:168
  311.3 3.5 all-to-all-start.12
  315.9 12.0 %all-to-all-done.12 = bf16[8,4,32,512]{3,2,0,1:T(8,128)(2,1)S(1)} async-done(((bf16[8,4,32,512]{3,2,0,1:T(8,128)(2,1)}), bf16[8,4,32,512]{3,2,0,1:T(8,128)(2,1)S(1)}, u32[]{:S(2)}, u32[]{:S(2)}) %all-to-all-start.12) | async-done | bytes 1048608 | tf_op jit(solution)/shard_map/all_to_all | solution.py:169
  327.9 4.2 all-to-all-start.8
  338.0 7.3 %all-to-all-done.8 = bf16[8,4,32,512]{3,2,0,1:T(8,128)(2,1)} async-done(((bf16[8,4,32,512]{3,2,0,1:T(8,128)(2,1)}), bf16[8,4,32,512]{3,2,0,1:T(8,128)(2,1)}, u32[]{:S(2)}, u32[]{:S(2)}) %all-to-all-start.8) | async-done | bytes 1048608 | tf_op jit(solution)/shard_map/all_to_all | solution.py:167
  349.8 29.7 %all_to_all.158 = bf16[8,128,512]{2,1,0:T(8,128)(2,1)S(1)} all-to-all(bf16[8,128,512]{2,1,0:T(8,128)(2,1)S(1)} %bitcast.168), channel_id=1, replica_groups=mesh['bucket'=4,'head'=8] {'head'}, dimensions={0} | all-to-all | bytes 2097152 | tf_op jit(solution)/shard_map/all_to_all | solution.py:173
  379.5 29.0 %all_to_all.159 = bf16[8,128,512]{2,1,0:T(8,128)(2,1)S(1)} all-to-all(bf16[8,128,512]{2,1,0:T(8,128)(2,1)S(1)} %bitcast.167), channel_id=1, replica_groups=mesh['bucket'=4,'head'=8] {'head'}, dimensions={0} | all-to-all | bytes 2097152 | tf_op jit(solution)/shard_map/all_to_all | solution.py:182
  408.5 3.6 all-to-all-start.13
  414.2 24.3 %all-to-all-done.13 = bf16[8,128,512]{2,1,0:T(8,128)(2,1)S(1)} async-done(((bf16[8,128,512]{2,1,0:T(8,128)(2,1)}), bf16[8,128,512]{2,1,0:T(8,128)(2,1)S(1)}, u32[]{:S(2)}, u32[]{:S(2)}) %all-to-all-start.13) | async-done | bytes 1048608 | tf_op jit(solution)/shard_map/all_to_all | solution.py:191
  (144 shorter events, 103.9 us)
Async XLA Ops:
  0.6 8.7 %copy-start.9 = (bf16[128,4096]{1,0:T(8,128)(2,1)S(1)}, bf16[128,4096]{1,0:T(8,128)(2,1)}, u32[]{:S(2)}) copy-start(bf16[128,4096]{1,0:T(8,128)(2,1)} %param.13) | copy-start | bytes 3145732
  3.0 32.9 %all-to-all-start = ((bf16[128,8,512]{2,0,1:T(8,128)(2,1)}), bf16[128,8,512]{2,0,1:T(8,128)(2,1)S(1)}, u32[]{:S(2)}, u32[]{:S(2)}) async-start(bf16[128,8,512]{2,0,1:T(8,128)(2,1)} %bitcast.113), calls=%async_computation | async-start | bytes 2097152 | tf_op jit(solution)/shard_map/all_to_all | solution.py:121
  35.9 30.1 %all-to-all-start.2 = ((bf16[128,8,512]{2,0,1:T(8,128)(2,1)}), bf16[128,8,512]{2,0,1:T(8,128)(2,1)S(1)}, u32[]{:S(2)}, u32[]{:S(2)}) async-start(bf16[128,8,512]{2,0,1:T(8,128)(2,1)} %bitcast.112), calls=%async_computation.2 | async-start | bytes 2097152 | tf_op jit(solution)/shard_map/all_to_all | solution.py:122
  39.5 60.9 %copy-start.14 = (s32[128]{0:T(128)S(1)}, s32[128]{0:T(128)}, u32[]{:S(2)}) copy-start(s32[128]{0:T(128)} %param.16) | copy-start | bytes 1540
  66.0 30.1 %all-to-all-start.4 = ((bf16[128,8,512]{2,0,1:T(8,128)(2,1)}), bf16[128,8,512]{2,0,1:T(8,128)(2,1)S(1)}, u32[]{:S(2)}, u32[]{:S(2)}) async-start(bf16[128,8,512]{2,0,1:T(8,128)(2,1)} %bitcast.160), calls=%async_computation.4 | async-start | bytes 2097152 | tf_op jit(solution)/shard_map/all_to_all | solution.py:124
  96.1 4.7 %copy-start.7 = (bf16[128,8,512]{2,0,1:T(8,128)(2,1)}, bf16[128,8,512]{2,0,1:T(8,128)(2,1)S(1)}, u32[]{:S(2)}) copy-start(bf16[128,8,512]{2,0,1:T(8,128)(2,1)S(1)} %all-to-all-done.4) | copy-start | bytes 3145732
  96.1 30.8 %all-to-all-start.6 = ((bf16[128,8,512]{2,0,1:T(8,128)(2,1)}), bf16[128,8,512]{2,0,1:T(8,128)(2,1)}, u32[]{:S(2)}, u32[]{:S(2)}) async-start(bf16[128,8,512]{2,0,1:T(8,128)(2,1)} %bitcast.158), calls=%async_computation.6 | async-start | bytes 2097152 | tf_op jit(solution)/shard_map/all_to_all | solution.py:123
  132.8 52.1 %copy-start.15 = (s32[128]{0:T(128)S(1)}, s32[128]{0:T(128)}, u32[]{:S(2)}) copy-start(s32[128]{0:T(128)} %param.17) | copy-start | bytes 1540
  166.2 14.4 %all-to-all-start.5 = ((bf16[8,4,32,512]{3,2,0,1:T(8,128)(2,1)}), bf16[8,4,32,512]{3,2,0,1:T(8,128)(2,1)S(1)}, u32[]{:S(2)}, u32[]{:S(2)}) async-start(bf16[8,4,32,512]{3,2,0,1:T(8,128)(2,1)} %get-tuple-element.199), calls=%async_computation.5 | async-start | bytes 2097152 | tf_op jit(solution)/shard_map/all_to_all | solution.py:148
  180.6 4.3 copy-start.6
  180.6 17.7 %all-to-all-start.7 = ((bf16[8,4,32,512]{3,2,0,1:T(8,128)(2,1)}), bf16[8,4,32,512]{3,2,0,1:T(8,128)(2,1)}, u32[]{:S(2)}, u32[]{:S(2)}) async-start(bf16[8,4,32,512]{3,2,0,1:T(8,128)(2,1)} %get-tuple-element.197), calls=%async_computation.7 | async-start | bytes 2097152 | tf_op jit(solution)/shard_map/all_to_all | solution.py:141
  209.6 9.1 %copy-start.4 = (bf16[32,32,512]{2,1,0:T(8,128)(2,1)S(1)}, bf16[32,32,512]{2,1,0:T(8,128)(2,1)}, u32[]{:S(2)}) copy-start(bf16[32,32,512]{2,1,0:T(8,128)(2,1)} %get-tuple-element.195) | copy-start | bytes 3145732
  231.7 4.1 copy-start.11
  235.8 1.9 copy-start
  240.8 3.5 copy-start.2
  240.8 3.7 copy-start.10
  244.6 1.3 copy-start.12
  244.6 2.7 copy-start.1
  246.3 1.0 copy-start.13
  261.5 4.1 copy-start.11
  265.6 1.9 copy-start
  270.6 3.5 copy-start.2
  270.6 3.7 copy-start.10
  274.3 1.3 copy-start.12
  274.3 2.7 copy-start.1
  294.0 5.2 %copy-start.5 = (bf16[32,32,512]{2,1,0:T(8,128)(2,1)S(1)}, bf16[32,32,512]{2,1,0:T(8,128)(2,1)}, u32[]{:S(2)}) copy-start(bf16[32,32,512]{2,1,0:T(8,128)(2,1)} %get-tuple-element.190) | copy-start | bytes 3145732
  294.0 20.8 %copy-start.3 = (bf16[32,32,512]{2,1,0:T(8,128)(2,1)S(1)}, bf16[32,32,512]{2,1,0:T(8,128)(2,1)}, u32[]{:S(2)}) copy-start(bf16[32,32,512]{2,1,0:T(8,128)(2,1)} %get-tuple-element.192) | copy-start | bytes 3145732
  295.0 16.3 %all-to-all-start.10 = ((bf16[8,4,32,512]{3,2,0,1:T(8,128)(2,1)}), bf16[8,4,32,512]{3,2,0,1:T(8,128)(2,1)S(1)}, u32[]{:S(2)}, u32[]{:S(2)}) async-start(bf16[8,4,32,512]{3,2,0,1:T(8,128)(2,1)} %copy.133), calls=%async_computation.10 | async-start | bytes 2097152 | tf_op jit(solution)/shard_map/all_to_all | solution.py:168
  311.3 16.6 %all-to-all-start.12 = ((bf16[8,4,32,512]{3,2,0,1:T(8,128)(2,1)}), bf16[8,4,32,512]{3,2,0,1:T(8,128)(2,1)S(1)}, u32[]{:S(2)}, u32[]{:S(2)}) async-start(bf16[8,4,32,512]{3,2,0,1:T(8,128)(2,1)} %copy.139), calls=%async_computation.12 | async-start | bytes 2097152 | tf_op jit(solution)/shard_map/all_to_all | solution.py:169
  327.9 17.4 %all-to-all-start.8 = ((bf16[8,4,32,512]{3,2,0,1:T(8,128)(2,1)}), bf16[8,4,32,512]{3,2,0,1:T(8,128)(2,1)}, u32[]{:S(2)}, u32[]{:S(2)}) async-start(bf16[8,4,32,512]{3,2,0,1:T(8,128)(2,1)} %copy.128), calls=%async_computation.8 | async-start | bytes 2097152 | tf_op jit(solution)/shard_map/all_to_all | solution.py:167
  336.4 10.7 %copy-start.8 = (bf16[32,32,512]{2,1,0:T(8,128)(2,1)S(1)}, bf16[32,32,512]{2,1,0:T(8,128)(2,1)}, u32[]{:S(2)}) copy-start(bf16[32,32,512]{2,1,0:T(8,128)(2,1)} %gather_fusion.11) | copy-start | bytes 3145732
  408.5 30.1 %all-to-all-start.13 = ((bf16[8,128,512]{2,1,0:T(8,128)(2,1)}), bf16[8,128,512]{2,1,0:T(8,128)(2,1)S(1)}, u32[]{:S(2)}, u32[]{:S(2)}) async-start(bf16[8,128,512]{2,1,0:T(8,128)(2,1)} %bitcast.164), calls=%async_computation.13 | async-start | bytes 2097152 | tf_op jit(solution)/shard_map/all_to_all | solution.py:191
  (1 other events, 1.0 us)
where the time goes:
time: 442 us; the launch traced here: 440 us
  waiting for transfers between devices  162 us (37%)
  blocking collectives  92.1 us (21%)
  local copies, waits for them, and re-layouts  77 us (17%)
  starting transfers between devices  40.9 us (9%)
  matrix products  39.6 us (9%)
  other arithmetic  25.5 us (6%)
    all_to_all x1, blocking collectives, shards(): lax.all_to_all(jnp.take_along_axis(home_q, seg_dest[:, :, None, None], ax...  29.7 us
    all_to_all x1, blocking collectives, shards(): lax.all_to_all(jnp.take_along_axis(home_k, seg_dest[:, :, None, None], ax...  29 us
    all_to_all x1, waiting for transfers between devices, shards(): lax.all_to_all(queries, 'head', split_axis=1, concat_axis=0, tiled=True)  25.5 us
    all_to_all x1, waiting for transfers between devices, shards(): lax.all_to_all(jnp.take_along_axis(home_v, seg_dest[:, :, None, None], ax...  24.3 us
    all_to_all x1, waiting for transfers between devices, shards(): lax.all_to_all(grad_out, 'head', split_axis=1, concat_axis=0, tiled=True)  24.2 us
    all_to_all x1, waiting for transfers between devices, shards(): lax.all_to_all(keys, 'head', split_axis=1, concat_axis=0, tiled=True)  24.2 us
    all_to_all x1, waiting for transfers between devices, shards(): lax.all_to_all(values, 'head', split_axis=1, concat_axis=0, tiled=True)  22.9 us
    all_to_all x1, blocking collectives, shards(): lax.all_to_all(group_segment(narrow_q, page_pick, n_head, n_bucket, page_...  17.6 us
  transfers between devices with their start and end apart: 10, of which 9 were waited for; matrix products, arithmetic and copies ran while one was open for 8% of the time, Pallas kernels for 0%

commit v1 on v0

v1 whole, which is shorter than its diff:
```python
import functools

import jax
import jax.numpy as jnp
from jax import lax
from jax.experimental import pallas as pl
from jax.experimental.pallas import tpu as pltpu
from jax.sharding import PartitionSpec as P

HD = 128
LOG2E = 1.4426950408889634
MESH = pl.DeviceIdType.MESH


def routing(page_dest, doc_start, bucket_index, head_index, n_bucket, n_head, block_slots):
    slots = n_bucket * n_head
    dest = page_dest.reshape(slots, n_bucket)
    dest_bucket = dest // slots
    arrival_slot = jnp.sum(jnp.where(dest_bucket == bucket_index, dest % slots, 0), axis=1)
    slot_range = jnp.arange(slots, dtype=jnp.int32)
    slot_order = jnp.sum(
        jnp.where(arrival_slot[:, None] == slot_range[None, :], slot_range[:, None], 0), axis=0
    )
    mine = lax.dynamic_index_in_dim(
        dest_bucket, bucket_index * n_head + head_index, 0, keepdims=False
    )
    page_range = jnp.arange(n_bucket, dtype=jnp.int32)
    pick = jnp.sum(jnp.where(mine[:, None] == page_range[None, :], page_range[:, None], 0), axis=0)
    starts = lax.dynamic_slice_in_dim(doc_start, bucket_index * slots, slots)
    starts = starts.reshape(slots // block_slots, block_slots)[:, 0]
    firsts = jnp.arange(slots // block_slots, dtype=jnp.int32) * block_slots
    hidden = jnp.where(firsts[None, :] >= starts[:, None], 0.0, -jnp.inf).astype(jnp.float32)
    return pick, mine, arrival_slot, slot_order, hidden.reshape(-1)


def dot_nt(a, b):
    return lax.dot_general(a, b, (((1,), (1,)), ((), ())), preferred_element_type=jnp.float32)


def dot(a, b):
    return jnp.dot(a, b, preferred_element_type=jnp.float32)


def kernel(
    n_bucket, n_head, heads, page, block,
    pick, mine, arrival, order, hidden,
    q_in, k_in, v_in, g_in,
    q_out, k_out, v_out,
    send, recv, back, home, stage, stage_back,
    q_s, k_s, v_s, g_s, k_t, dq, dk, dv, dk_sum, dv_sum,
    send_sem, recv_sem, back_sem, home_sem,
):
    n = n_bucket * n_head
    me = lax.axis_index("bucket") * n_head + lax.axis_index("head")
    seg = n * page
    blocks = seg // block
    scale = float(HD) ** (-0.5)

    barrier = pltpu.get_barrier_semaphore()

    @pl.loop(1, n)
    def _(step):
        d = lax.rem(me + step, n)
        pl.semaphore_signal(
            barrier, inc=1, device_id=(d // n_head, lax.rem(d, n_head)), device_id_type=MESH
        )

    def pack(h, d, where):
        from_page = pick[d // n_head]
        column = pl.multiple_of((lax.rem(d, n_head) * heads + h) * HD, HD)
        for a, src in enumerate((q_in, k_in, v_in, g_in)):
            where[h, d, pl.ds(a * page, page), :] = src[from_page, :, pl.ds(column, HD)]

    pl.semaphore_wait(barrier, n - 1)

    @pl.loop(0, heads)
    def _(h):
        @pl.loop(1, n)
        def _(step):
            d = lax.rem(me + step, n)
            pack(h, d, send)
            pltpu.make_async_remote_copy(
                src_ref=send.at[h, d],
                dst_ref=recv.at[h, me],
                send_sem=send_sem.at[h],
                recv_sem=recv_sem.at[h],
                device_id=(d // n_head, lax.rem(d, n_head)),
                device_id_type=MESH,
            ).start()

        pack(h, me, recv)

    key_row = lax.broadcasted_iota(jnp.int32, (block, block), 0)
    query_col = lax.broadcasted_iota(jnp.int32, (block, block), 1)
    causal = key_row <= query_col

    def attend(i):
        rows = (i + 1) * block
        here = pl.ds(i * block, block)
        q_b = q_s[here, :]
        g_b = g_s[here, :]
        s = dot_nt(k_s[pl.ds(0, rows), :], q_b)
        parts = []
        for j in range(i):
            parts.append(s[j * block : (j + 1) * block] + hidden[i * blocks + j])
        parts.append(jnp.where(causal, s[i * block :], -jnp.inf))
        s = jnp.concatenate(parts, axis=0) if i else parts[0]
        top = jnp.max(s, axis=0, keepdims=True)
        w = jnp.exp2((s - top) * (scale * LOG2E))
        p = (w * (1.0 / jnp.sum(w, axis=0, keepdims=True))).astype(jnp.bfloat16)
        gp = dot_nt(v_s[pl.ds(0, rows), :], g_b)
        p32 = p.astype(jnp.float32)
        row_dot = jnp.sum(p32 * gp, axis=0, keepdims=True)
        gs = (p32 * ((gp - row_dot) * scale)).astype(jnp.bfloat16)
        if i == blocks - 1:
            dv_sum[...] = dot(p, g_b)
            dk_sum[...] = dot(gs, q_b)
        else:
            dv_sum[pl.ds(0, rows), :] += dot(p, g_b)
            dk_sum[pl.ds(0, rows), :] += dot(gs, q_b)
        gq = dot(k_t[:, pl.ds(0, rows)], gs).T.reshape(block // page, page, HD)
        dq[pl.ds(i * (block // page), block // page)] = gq.astype(jnp.bfloat16)

    def wait_all(ref, h, sem):
        part = ref.at[h, pl.ds(0, n - 1)]
        pltpu.make_async_copy(part, part, sem.at[h]).wait()

    def pack_back(h, d, at, where):
        slot = arrival[d]
        for a, src in enumerate((dq, dk, dv)):
            where[h, at, pl.ds(a * page, page), :] = src[slot]

    @pl.loop(0, heads)
    def _(h):
        wait_all(recv, h, recv_sem)

        @pl.loop(0, n)
        def _(s):
            stage[s] = recv[h, s]

        @pl.loop(0, n)
        def _(s):
            src = order[s]
            to = pl.ds(pl.multiple_of(s * page, page), page)
            for a, dst in enumerate((q_s, k_s, v_s, g_s)):
                dst[to, :] = stage[src, pl.ds(a * page, page), :]

        k_t[...] = k_s[...].T
        for i in reversed(range(blocks)):
            attend(i)
        dk[...] = dk_sum[...].reshape(n, page, HD).astype(jnp.bfloat16)
        dv[...] = dv_sum[...].reshape(n, page, HD).astype(jnp.bfloat16)

        @pl.loop(1, n)
        def _(step):
            d = lax.rem(me + step, n)
            pack_back(h, d, d, back)
            pltpu.make_async_remote_copy(
                src_ref=back.at[h, d],
                dst_ref=home.at[h, me],
                send_sem=back_sem.at[h],
                recv_sem=home_sem.at[h],
                device_id=(d // n_head, lax.rem(d, n_head)),
                device_id_type=MESH,
            ).start()

        pack_back(h, me, me, home)

    @pl.loop(0, heads)
    def _(h):
        wait_all(home, h, home_sem)

        @pl.loop(0, n)
        def _(s):
            stage_back[s] = home[h, s]

        @pl.loop(0, n)
        def _(t):
            p = t // n_head
            group = lax.rem(t, n_head)
            src = mine[p] * n_head + group
            to = pl.ds(pl.multiple_of(p * page, page), page)
            column = pl.ds(pl.multiple_of((group * heads + h) * HD, HD), HD)
            for a, dst in enumerate((q_out, k_out, v_out)):
                dst[to, column] = stage_back[src, pl.ds(a * page, page), :]

    @pl.loop(0, heads)
    def _(h):
        wait_all(send, h, send_sem)
        wait_all(back, h, back_sem)


def shards(queries, keys, values, grad_out, page_dest, doc_start):
    n_bucket = lax.axis_size("bucket")
    n_head = lax.axis_size("head")
    n = n_bucket * n_head
    tok_dev, width = queries.shape
    page = tok_dev // n_bucket
    heads = width // n_head // HD
    seg = n * page
    block_slots = 2 * n_bucket
    block = block_slots * page
    tables = routing(
        page_dest, doc_start, lax.axis_index("bucket"), lax.axis_index("head"),
        n_bucket, n_head, block_slots,
    )
    low = jnp.bfloat16
    back_rows = -(-3 * page // 16) * 16
    smem = pl.BlockSpec(memory_space=pltpu.SMEM)
    vmem = pl.BlockSpec(memory_space=pltpu.VMEM)
    pairs = heads * seg * seg // 2
    return pl.pallas_call(
        functools.partial(kernel, n_bucket, n_head, heads, page, block),
        out_shape=[jax.ShapeDtypeStruct((tok_dev, width), low)] * 3,
        in_specs=[smem] * 5 + [vmem] * 4,
        out_specs=[vmem] * 3,
        scratch_shapes=[
            pltpu.VMEM((heads, n, 4 * page, HD), low),
            pltpu.VMEM((heads, n, 4 * page, HD), low),
            pltpu.VMEM((heads, n, back_rows, HD), low),
            pltpu.VMEM((heads, n, back_rows, HD), low),
            pltpu.VMEM((n, 4 * page, HD), low),
            pltpu.VMEM((n, back_rows, HD), low),
            pltpu.VMEM((seg, HD), low),
            pltpu.VMEM((seg, HD), low),
            pltpu.VMEM((seg, HD), low),
            pltpu.VMEM((seg, HD), low),
            pltpu.VMEM((HD, seg), low),
            pltpu.VMEM((n, page, HD), low),
            pltpu.VMEM((n, page, HD), low),
            pltpu.VMEM((n, page, HD), low),
            pltpu.VMEM((seg, HD), jnp.float32),
            pltpu.VMEM((seg, HD), jnp.float32),
            pltpu.SemaphoreType.DMA((heads,)),
            pltpu.SemaphoreType.DMA((heads,)),
            pltpu.SemaphoreType.DMA((heads,)),
            pltpu.SemaphoreType.DMA((heads,)),
        ],
        compiler_params=pltpu.CompilerParams(
            collective_id=0, has_side_effects=True, vmem_limit_bytes=56 * 1024 * 1024
        ),
        cost_estimate=pl.CostEstimate(
            flops=10 * pairs * HD, bytes_accessed=14 * tok_dev * width, transcendentals=pairs
        ),
    )(*tables, *(a.reshape(n_bucket, page, width) for a in (queries, keys, values, grad_out)))


def solution(mesh):
    split = P(("bucket", "head"), None)
    return jax.shard_map(
        shards,
        mesh=mesh,
        in_specs=(split, split, split, split, P(), P()),
        out_specs=(split, split, split),
        check_vma=False,
    )
```

time: 442 us -> 179 us (0.40)
  Pallas kernels: 0 us -> 170 us
  waiting for transfers between devices: 162 us -> 0 us
  blocking collectives: 92.1 us -> 0 us
  local copies, waits for them, and re-layouts: 77 us -> 6.65 us
  starting transfers between devices: 40.9 us -> 0 us
  matrix products: 39.6 us -> 0 us
  other arithmetic: 25.5 us -> 1.37 us
    pallas_call x0 -> x1, Pallas kernels: none -> 170 us  [shards(): pl.pallas_call(functools.partial(kernel, n_bucket, n_head, heads, page, b...]
    all_to_all x10 -> x0, waiting for transfers between devices: 162 us -> none  [the longest x1 25.5 us: shards(): lax.all_to_all(queries, 'head', split_axis=1, concat_axis=0, tiled=True)]
    all_to_all x4 -> x0, blocking collectives: 92.1 us -> none  [the longest x1 29.7 us: shards(): lax.all_to_all(jnp.take_along_axis(home_q, seg_dest[:, :, None, None], ax...]
    all_to_all x10 -> x0, starting transfers between devices: 40.9 us -> none  [the longest x1 6.33 us: shards(): lax.all_to_all(queries, 'head', split_axis=1, concat_axis=0, tiled=True)]
    gather x18 -> x0, local copies, waits for them, and re-layouts: 25.8 us -> none  [the longest x4 10.3 us: to_slots(): jnp.take(shaped, slot_order, axis=0)]
    dot_general x10 -> x0, matrix products: 24.5 us -> none  [the longest x2 7.04 us: one_block(): jnp.einsum('hqk,qhd->khd', grad_score, query_blk, preferred_element_type=...]
    all_to_all x13 -> x0, local copies, waits for them, and re-layouts: 20.4 us -> none  [the longest x1 2.38 us: shards(): lax.all_to_all(queries, 'head', split_axis=1, concat_axis=0, tiled=True)]
    sub x2 -> x0, matrix products: 15.1 us -> none  [one_block(): weights = jnp.exp(scores - row_top)]
  transfers between devices with their start and end apart: 10 -> 0, of which waited for: 9 -> 0; matrix products, arithmetic and copies ran while one was open for 8% -> 0% of each run, Pallas kernels for 0% -> 0%
where the time goes in v1:
time: 179 us
  Pallas kernels  170 us (95%)
  local copies, waits for them, and re-layouts  6.65 us (4%)
    pallas_call x1, Pallas kernels, shards(): pl.pallas_call(functools.partial(kernel, n_bucket, n_head, heads, page, b...  170 us
    unnamed x15, local copies, waits for them, and re-layouts  5.66 us

profile of v1, /device:TPU:0, one launch (start us, length us, event | category | flops | bytes accessed | tf_op | source)
XLA Modules:
  0.0 178.8 jit_solution(9406553352101994351)
XLA Ops:
  0.6 0.0 copy-start.4
  0.7 0.6 copy-done.4
  1.3 0.1 dynamic_slice.8
  1.4 0.1 reshape.39
  1.5 0.1 slice_reduce_fusion
  1.6 0.1 compare_select_fusion
  1.6 0.0 copy-start.3
  1.7 0.6 select_n.47.hidden
  2.3 0.0 copy-done.3
  2.3 0.1 reshape.38
  2.4 0.1 fusion.1
  2.5 0.0 copy-start.2
  2.6 0.0 copy-start.5
  2.6 0.6 select_reduce_fusion.1.pick
  3.2 0.0 copy-done.2
  3.2 0.0 copy-done.5
  3.2 0.6 select_reduce_fusion.order
  3.7 170.1 %shard_map.85 = (bf16[128,4096]{1,0:T(8,128)(2,1)}, bf16[128,4096]{1,0:T(8,128)(2,1)}, bf16[128,4096]{1,0:T(8,128)(2,1)}) custom-call(s32[4]{0:T(128)} %select_reduce_fusion.1.pick, s32[4]{0:T(128)} %copy-done.5, s32[32]{0:T(128)} %copy-done.2, s32[32]{0:T(128)} %select_reduce_fusion.order, f32[16]{0:T(128)} %select_n.47.hidden, ...), custom_call_target="tpu_custom_call" | custom-call | flops 2684354560 | bytes 7340032 | tf_op jit(solution)/shard_map/pallas_call | solution.py:212
  173.9 0.0 copy-start.1
  173.9 2.4 %copy.12 = bf16[128,4096]{1,0:T(8,128)(2,1)} copy(bf16[128,4096]{1,0:T(8,128)(2,1)} %get-tuple-element.8) | data formatting | bytes 2097152
  176.2 0.0 copy-done.1
  176.2 0.0 copy-start
  176.2 1.0 copy.13
  177.2 0.6 copy-done
  177.8 1.0 copy.14
  (2 shorter events, 0.0 us)
Async XLA Ops:
  0.6 0.7 copy-start.4
  1.6 0.7 copy-start.3
  2.5 0.6 copy-start.2
  2.6 0.6 copy-start.5
  173.9 2.4 %copy-start.1 = (bf16[128,4096]{1,0:T(8,128)(2,1)S(1)}, bf16[128,4096]{1,0:T(8,128)(2,1)}, u32[]{:S(2)}) copy-start(bf16[128,4096]{1,0:T(8,128)(2,1)} %get-tuple-element.9) | copy-start | bytes 3145732
  176.2 1.6 copy-start

commit v2 on v1

--- a/solution.py
+++ b/solution.py
@@ -29,8 +29,8 @@
     starts = lax.dynamic_slice_in_dim(doc_start, bucket_index * slots, slots)
     starts = starts.reshape(slots // block_slots, block_slots)[:, 0]
     firsts = jnp.arange(slots // block_slots, dtype=jnp.int32) * block_slots
-    hidden = jnp.where(firsts[None, :] >= starts[:, None], 0.0, -jnp.inf).astype(jnp.float32)
-    return pick, mine, arrival_slot, slot_order, hidden.reshape(-1)
+    hidden = (firsts[None, :] < starts[:, None]).astype(jnp.int32)
+    return jnp.concatenate([pick, mine, arrival_slot, slot_order, hidden.reshape(-1)])
 
 
 def dot_nt(a, b):
@@ -43,7 +43,7 @@
 
 def kernel(
     n_bucket, n_head, heads, page, block,
-    pick, mine, arrival, order, hidden,
+    table,
     q_in, k_in, v_in, g_in,
     q_out, k_out, v_out,
     send, recv, back, home, stage, stage_back,
@@ -56,6 +56,11 @@
     blocks = seg // block
     scale = float(HD) ** (-0.5)
 
+    mine_at = n_bucket
+    arrival_at = 2 * n_bucket
+    order_at = arrival_at + n
+    hidden_at = order_at + n
+
     barrier = pltpu.get_barrier_semaphore()
 
     @pl.loop(1, n)
@@ -66,7 +71,7 @@
         )
 
     def pack(h, d, where):
-        from_page = pick[d // n_head]
+        from_page = table[d // n_head]
         column = pl.multiple_of((lax.rem(d, n_head) * heads + h) * HD, HD)
         for a, src in enumerate((q_in, k_in, v_in, g_in)):
             where[h, d, pl.ds(a * page, page), :] = src[from_page, :, pl.ds(column, HD)]
@@ -102,7 +107,8 @@
         s = dot_nt(k_s[pl.ds(0, rows), :], q_b)
         parts = []
         for j in range(i):
-            parts.append(s[j * block : (j + 1) * block] + hidden[i * blocks + j])
+            lower = table[hidden_at + i * blocks + j].astype(jnp.float32) * -3e38
+            parts.append(s[j * block : (j + 1) * block] + lower)
         parts.append(jnp.where(causal, s[i * block :], -jnp.inf))
         s = jnp.concatenate(parts, axis=0) if i else parts[0]
         top = jnp.max(s, axis=0, keepdims=True)
@@ -126,35 +132,14 @@
         pltpu.make_async_copy(part, part, sem.at[h]).wait()
 
     def pack_back(h, d, at, where):
-        slot = arrival[d]
+        slot = table[arrival_at + d]
         for a, src in enumerate((dq, dk, dv)):
             where[h, at, pl.ds(a * page, page), :] = src[slot]
 
-    @pl.loop(0, heads)
-    def _(h):
-        wait_all(recv, h, recv_sem)
-
-        @pl.loop(0, n)
-        def _(s):
-            stage[s] = recv[h, s]
-
-        @pl.loop(0, n)
-        def _(s):
-            src = order[s]
-            to = pl.ds(pl.multiple_of(s * page, page), page)
-            for a, dst in enumerate((q_s, k_s, v_s, g_s)):
-                dst[to, :] = stage[src, pl.ds(a * page, page), :]
-
-        k_t[...] = k_s[...].T
-        for i in reversed(range(blocks)):
-            attend(i)
-        dk[...] = dk_sum[...].reshape(n, page, HD).astype(jnp.bfloat16)
-        dv[...] = dv_sum[...].reshape(n, page, HD).astype(jnp.bfloat16)
-
+    def send_back(h):
         @pl.loop(1, n)
         def _(step):
             d = lax.rem(me + step, n)
-            pack_back(h, d, d, back)
             pltpu.make_async_remote_copy(
                 src_ref=back.at[h, d],
                 dst_ref=home.at[h, me],
@@ -164,7 +149,41 @@
                 device_id_type=MESH,
             ).start()
 
+    @pl.loop(0, heads)
+    def _(h):
+        wait_all(recv, h, recv_sem)
+
+        @pl.when(h == heads - 1)
+        def _():
+            @pl.loop(0, heads - 1)
+            def _(done):
+                send_back(done)
+
+        @pl.loop(0, n)
+        def _(s):
+            stage[s] = recv[h, s]
+
+        @pl.loop(0, n)
+        def _(s):
+            src = table[order_at + s]
+            to = pl.ds(pl.multiple_of(s * page, page), page)
+            for a, dst in enumerate((q_s, k_s, v_s, g_s)):
+                dst[to, :] = stage[src, pl.ds(a * page, page), :]
+
+        k_t[...] = k_s[...].T
+        for i in reversed(range(blocks)):
+            attend(i)
+        dk[...] = dk_sum[...].reshape(n, page, HD).astype(jnp.bfloat16)
+        dv[...] = dv_sum[...].reshape(n, page, HD).astype(jnp.bfloat16)
+
+        @pl.loop(1, n)
+        def _(step):
+            d = lax.rem(me + step, n)
+            pack_back(h, d, d, back)
+
         pack_back(h, me, me, home)
+
+    send_back(heads - 1)
 
     @pl.loop(0, heads)
     def _(h):
@@ -178,7 +197,7 @@
         def _(t):
             p = t // n_head
             group = lax.rem(t, n_head)
-            src = mine[p] * n_head + group
+            src = table[mine_at + p] * n_head + group
             to = pl.ds(pl.multiple_of(p * page, page), page)
             column = pl.ds(pl.multiple_of((group * heads + h) * HD, HD), HD)
             for a, dst in enumerate((q_out, k_out, v_out)):
@@ -200,7 +219,7 @@
     seg = n * page
     block_slots = 2 * n_bucket
     block = block_slots * page
-    tables = routing(
+    table = routing(
         page_dest, doc_start, lax.axis_index("bucket"), lax.axis_index("head"),
         n_bucket, n_head, block_slots,
     )
@@ -212,7 +231,7 @@
     return pl.pallas_call(
         functools.partial(kernel, n_bucket, n_head, heads, page, block),
         out_shape=[jax.ShapeDtypeStruct((tok_dev, width), low)] * 3,
-        in_specs=[smem] * 5 + [vmem] * 4,
+        in_specs=[smem] + [vmem] * 4,
         out_specs=[vmem] * 3,
         scratch_shapes=[
             pltpu.VMEM((heads, n, 4 * page, HD), low),
@@ -242,7 +261,7 @@
         cost_estimate=pl.CostEstimate(
             flops=10 * pairs * HD, bytes_accessed=14 * tok_dev * width, transcendentals=pairs
         ),
-    )(*tables, *(a.reshape(n_bucket, page, width) for a in (queries, keys, values, grad_out)))
+    )(table, *(a.reshape(n_bucket, page, width) for a in (queries, keys, values, grad_out)))
 
 
 def solution(mesh):

time: 179 us -> 180 us (level)
    unnamed x15 -> x11, local copies, waits for them, and re-layouts: 5.66 us -> 6.17 us
where the time goes in v2:
time: 180 us
  Pallas kernels  171 us (95%)
  local copies, waits for them, and re-layouts  7.23 us (4%)
    pallas_call x1, Pallas kernels, shards(): pl.pallas_call(functools.partial(kernel, n_bucket, n_head, heads, page, b...  171 us
    unnamed x11, local copies, waits for them, and re-layouts  6.17 us

profile of v2, /device:TPU:0, one launch (start us, length us, event | category | flops | bytes accessed | tf_op | source)
XLA Modules:
  0.0 179.6 jit_solution(16711695246358351378)
XLA Ops:
  0.6 0.0 copy-start.3
  0.7 0.6 copy-done.3
  1.3 0.1 dynamic_slice.8
  1.4 0.1 reshape.38
  1.5 0.1 slice_reduce_fusion
  1.6 0.1 compare_convert_fusion
  1.6 0.0 copy-start.2
  1.7 0.1 reshape.43
  1.7 0.6 copy-done.2
  2.3 0.1 reshape.37
  2.4 0.1 fusion.1
  2.6 0.1 select_reduce_fusion.1
  2.6 0.1 select_reduce_fusion
  2.7 0.6 concatenate.3.table
  3.3 171.3 %shard_map.85 = (bf16[128,4096]{1,0:T(8,128)(2,1)}, bf16[128,4096]{1,0:T(8,128)(2,1)}, bf16[128,4096]{1,0:T(8,128)(2,1)}) custom-call(s32[88]{0:T(128)} %concatenate.3.table, bf16[4,32,4096]{2,1,0:T(8,128)(2,1)} %bitcast.6, bf16[4,32,4096]{2,1,0:T(8,128)(2,1)} %bitcast.7, bf16[4,32,4096]{2,1,0:T(8,128)(2,1)} %bitcast.8, bf16[4,32,4096]{2,1,0:T(8,128)(2,1)} %bitcast.9), custom_call_target="tpu_custom_call" | custom-call | flops 2684354560 | bytes 7340032 | tf_op jit(solution)/shard_map/pallas_call | solution.py:231
  174.7 0.0 copy-start.1
  174.7 2.4 %copy.12 = bf16[128,4096]{1,0:T(8,128)(2,1)} copy(bf16[128,4096]{1,0:T(8,128)(2,1)} %get-tuple-element.8) | data formatting | bytes 2097152
  177.0 0.0 copy-done.1
  177.0 0.0 copy-start
  177.0 1.0 copy.13
  178.0 0.6 copy-done
  178.6 1.0 copy.14
  (2 shorter events, 0.0 us)
Async XLA Ops:
  0.6 0.7 copy-start.3
  1.6 0.7 copy-start.2
  174.7 2.4 %copy-start.1 = (bf16[128,4096]{1,0:T(8,128)(2,1)S(1)}, bf16[128,4096]{1,0:T(8,128)(2,1)}, u32[]{:S(2)}) copy-start(bf16[128,4096]{1,0:T(8,128)(2,1)} %get-tuple-element.9) | copy-start | bytes 3145732
  177.0 1.6 copy-start

commit v3 on v1

--- a/solution.py
+++ b/solution.py
@@ -29,8 +29,8 @@
     starts = lax.dynamic_slice_in_dim(doc_start, bucket_index * slots, slots)
     starts = starts.reshape(slots // block_slots, block_slots)[:, 0]
     firsts = jnp.arange(slots // block_slots, dtype=jnp.int32) * block_slots
-    hidden = jnp.where(firsts[None, :] >= starts[:, None], 0.0, -jnp.inf).astype(jnp.float32)
-    return pick, mine, arrival_slot, slot_order, hidden.reshape(-1)
+    hidden = (firsts[None, :] < starts[:, None]).astype(jnp.int32)
+    return mine, jnp.concatenate([pick, arrival_slot, slot_order, hidden.reshape(-1)])
 
 
 def dot_nt(a, b):
@@ -43,12 +43,13 @@
 
 def kernel(
     n_bucket, n_head, heads, page, block,
-    pick, mine, arrival, order, hidden,
+    table,
+    q_hbm, k_hbm, v_hbm, g_hbm,
+    home,
     q_in, k_in, v_in, g_in,
-    q_out, k_out, v_out,
-    send, recv, back, home, stage, stage_back,
+    send, recv, back, stage,
     q_s, k_s, v_s, g_s, k_t, dq, dk, dv, dk_sum, dv_sum,
-    send_sem, recv_sem, back_sem, home_sem,
+    send_sem, recv_sem, back_sem, home_sem, own_sem, load_sem,
 ):
     n = n_bucket * n_head
     me = lax.axis_index("bucket") * n_head + lax.axis_index("head")
@@ -56,6 +57,19 @@
     blocks = seg // block
     scale = float(HD) ** (-0.5)
 
+    arrival_at = n_bucket
+    order_at = arrival_at + n
+    hidden_at = order_at + n
+
+    loads = [
+        pltpu.make_async_copy(src, dst, load_sem.at[a])
+        for a, (src, dst) in enumerate(
+            ((q_hbm, q_in), (k_hbm, k_in), (v_hbm, v_in), (g_hbm, g_in))
+        )
+    ]
+    for load in loads:
+        load.start()
+
     barrier = pltpu.get_barrier_semaphore()
 
     @pl.loop(1, n)
@@ -66,12 +80,14 @@
         )
 
     def pack(h, d, where):
-        from_page = pick[d // n_head]
+        from_page = table[d // n_head]
         column = pl.multiple_of((lax.rem(d, n_head) * heads + h) * HD, HD)
         for a, src in enumerate((q_in, k_in, v_in, g_in)):
             where[h, d, pl.ds(a * page, page), :] = src[from_page, :, pl.ds(column, HD)]
 
     pl.semaphore_wait(barrier, n - 1)
+    for load in loads:
+        load.wait()
 
     @pl.loop(0, heads)
     def _(h):
@@ -102,7 +118,8 @@
         s = dot_nt(k_s[pl.ds(0, rows), :], q_b)
         parts = []
         for j in range(i):
-            parts.append(s[j * block : (j + 1) * block] + hidden[i * blocks + j])
+            lower = table[hidden_at + i * blocks + j].astype(jnp.float32) * -3e38
+            parts.append(s[j * block : (j + 1) * block] + lower)
         parts.append(jnp.where(causal, s[i * block :], -jnp.inf))
         s = jnp.concatenate(parts, axis=0) if i else parts[0]
         top = jnp.max(s, axis=0, keepdims=True)
@@ -125,10 +142,10 @@
         part = ref.at[h, pl.ds(0, n - 1)]
         pltpu.make_async_copy(part, part, sem.at[h]).wait()
 
-    def pack_back(h, d, at, where):
-        slot = arrival[d]
+    def pack_back(h, d):
+        slot = table[arrival_at + d]
         for a, src in enumerate((dq, dk, dv)):
-            where[h, at, pl.ds(a * page, page), :] = src[slot]
+            back[h, d, pl.ds(a * page, page), :] = src[slot]
 
     @pl.loop(0, heads)
     def _(h):
@@ -140,7 +157,7 @@
 
         @pl.loop(0, n)
         def _(s):
-            src = order[s]
+            src = table[order_at + s]
             to = pl.ds(pl.multiple_of(s * page, page), page)
             for a, dst in enumerate((q_s, k_s, v_s, g_s)):
                 dst[to, :] = stage[src, pl.ds(a * page, page), :]
@@ -154,7 +171,7 @@
         @pl.loop(1, n)
         def _(step):
             d = lax.rem(me + step, n)
-            pack_back(h, d, d, back)
+            pack_back(h, d)
             pltpu.make_async_remote_copy(
                 src_ref=back.at[h, d],
                 dst_ref=home.at[h, me],
@@ -164,30 +181,23 @@
                 device_id_type=MESH,
             ).start()
 
-        pack_back(h, me, me, home)
+        pack_back(h, me)
+        pltpu.make_async_copy(back.at[h, me], home.at[h, me], own_sem.at[h]).start()
 
     @pl.loop(0, heads)
     def _(h):
         wait_all(home, h, home_sem)
-
-        @pl.loop(0, n)
-        def _(s):
-            stage_back[s] = home[h, s]
-
-        @pl.loop(0, n)
-        def _(t):
-            p = t // n_head
-            group = lax.rem(t, n_head)
-            src = mine[p] * n_head + group
-            to = pl.ds(pl.multiple_of(p * page, page), page)
-            column = pl.ds(pl.multiple_of((group * heads + h) * HD, HD), HD)
-            for a, dst in enumerate((q_out, k_out, v_out)):
-                dst[to, column] = stage_back[src, pl.ds(a * page, page), :]
-
-    @pl.loop(0, heads)
-    def _(h):
+        pltpu.make_async_copy(back.at[h, me], home.at[h, me], own_sem.at[h]).wait()
         wait_all(send, h, send_sem)
         wait_all(back, h, back_sem)
+
+
+def deliver(heads, page, mine, home, q_out, k_out, v_out):
+    for p in range(mine.shape[0]):
+        bucket = mine[p]
+        for h in range(heads):
+            for a, dst in enumerate((q_out, k_out, v_out)):
+                dst[p, :, pl.ds(h * HD, HD)] = home[h, bucket, 0, pl.ds(a * page, page), :]
 
 
 def shards(queries, keys, values, grad_out, page_dest, doc_start):
@@ -200,27 +210,29 @@
     seg = n * page
     block_slots = 2 * n_bucket
     block = block_slots * page
-    tables = routing(
+    mine, table = routing(
         page_dest, doc_start, lax.axis_index("bucket"), lax.axis_index("head"),
         n_bucket, n_head, block_slots,
     )
     low = jnp.bfloat16
     back_rows = -(-3 * page // 16) * 16
     smem = pl.BlockSpec(memory_space=pltpu.SMEM)
-    vmem = pl.BlockSpec(memory_space=pltpu.VMEM)
+    hbm = pl.BlockSpec(memory_space=pl.ANY)
     pairs = heads * seg * seg // 2
-    return pl.pallas_call(
+    home = pl.pallas_call(
         functools.partial(kernel, n_bucket, n_head, heads, page, block),
-        out_shape=[jax.ShapeDtypeStruct((tok_dev, width), low)] * 3,
-        in_specs=[smem] * 5 + [vmem] * 4,
-        out_specs=[vmem] * 3,
+        out_shape=jax.ShapeDtypeStruct((heads, n, back_rows, HD), low),
+        in_specs=[smem] + [hbm] * 4,
+        out_specs=hbm,
         scratch_shapes=[
+            pltpu.VMEM((n_bucket, page, width), low),
+            pltpu.VMEM((n_bucket, page, width), low),
+            pltpu.VMEM((n_bucket, page, width), low),
+            pltpu.VMEM((n_bucket, page, width), low),
             pltpu.VMEM((heads, n, 4 * page, HD), low),
             pltpu.VMEM((heads, n, 4 * page, HD), low),
             pltpu.VMEM((heads, n, back_rows, HD), low),
-            pltpu.VMEM((heads, n, back_rows, HD), low),
             pltpu.VMEM((n, 4 * page, HD), low),
-            pltpu.VMEM((n, back_rows, HD), low),
             pltpu.VMEM((seg, HD), low),
             pltpu.VMEM((seg, HD), low),
             pltpu.VMEM((seg, HD), low),
@@ -235,6 +247,8 @@
             pltpu.SemaphoreType.DMA((heads,)),
             pltpu.SemaphoreType.DMA((heads,)),
             pltpu.SemaphoreType.DMA((heads,)),
+            pltpu.SemaphoreType.DMA((heads,)),
+            pltpu.SemaphoreType.DMA((4,)),
         ],
         compiler_params=pltpu.CompilerParams(
             collective_id=0, has_side_effects=True, vmem_limit_bytes=56 * 1024 * 1024
@@ -242,7 +256,18 @@
         cost_estimate=pl.CostEstimate(
             flops=10 * pairs * HD, bytes_accessed=14 * tok_dev * width, transcendentals=pairs
         ),
-    )(*tables, *(a.reshape(n_bucket, page, width) for a in (queries, keys, values, grad_out)))
+    )(table, *(a.reshape(n_bucket, page, width) for a in (queries, keys, values, grad_out)))
+    outs = pl.pallas_call(
+        functools.partial(deliver, heads, page),
+        grid=(n_head,),
+        out_shape=[jax.ShapeDtypeStruct((n_bucket, page, width), low)] * 3,
+        in_specs=[
+            smem,
+            pl.BlockSpec((heads, n_bucket, 1, back_rows, HD), lambda g: (0, 0, g, 0, 0)),
+        ],
+        out_specs=[pl.BlockSpec((n_bucket, page, heads * HD), lambda g: (0, 0, g))] * 3,
+    )(mine, home.reshape(heads, n_bucket, n_head, back_rows, HD))
+    return tuple(a.reshape(tok_dev, width) for a in outs)
 
 
 def solution(mesh):

time: 179 us -> 176 us (0.983)
  local copies, waits for them, and re-layouts: 6.65 us -> 1.78 us
  Pallas kernels: 170 us -> 172 us
    pallas_call x0 -> x1, Pallas kernels: none -> 6.33 us  [shards(): pl.pallas_call(functools.partial(deliver, heads, page), grid=(n_head,), o...]
    unnamed x15 -> x2, local copies, waits for them, and re-layouts: 5.66 us -> 0.01 us
    pallas_call x1, Pallas kernels: 170 us -> 166 us  [shards(): pl.pallas_call(functools.partial(kernel, n_bucket, n_head, heads, page, b...]
where the time goes in v3:
time: 176 us
  Pallas kernels  172 us (98%)
  local copies, waits for them, and re-layouts  1.78 us (1%)
    pallas_call x1, Pallas kernels, shards(): pl.pallas_call(functools.partial(kernel, n_bucket, n_head, heads, page, b...  166 us
    pallas_call x1, Pallas kernels, shards(): pl.pallas_call(functools.partial(deliver, heads, page), grid=(n_head,), o...  6.33 us

profile of v3, /device:TPU:0, one launch (start us, length us, event | category | flops | bytes accessed | tf_op | source)
XLA Modules:
  0.0 175.6 jit_solution(8398684856319455281)
XLA Ops:
  0.6 0.7 dynamic_slice.8
  1.4 0.1 reshape.50
  1.5 0.1 slice_reduce_fusion
  1.6 0.1 compare_convert_fusion
  1.7 0.1 reshape.59
  1.7 0.8 reshape.49
  2.5 0.1 fusion.1
  2.6 0.0 copy-start
  2.7 0.1 select_reduce_fusion.1
  2.7 0.1 select_reduce_fusion
  2.8 0.6 pad_add_fusion.table
  3.4 165.8 %shard_map.85 = bf16[4,32,96,128]{3,2,1,0:T(8,128)(2,1)} custom-call(s32[84]{0:T(128)} %pad_add_fusion.table, bf16[4,32,4096]{2,1,0:T(8,128)(2,1)} %bitcast.11, bf16[4,32,4096]{2,1,0:T(8,128)(2,1)} %bitcast.12, bf16[4,32,4096]{2,1,0:T(8,128)(2,1)} %bitcast.13, bf16[4,32,4096]{2,1,0:T(8,128)(2,1)} %bitcast.14), custom_call_target="tpu_custom_call" | custom-call | flops 2684354560 | bytes 7340032 | tf_op jit(solution)/shard_map/pallas_call | solution.py:222
  169.2 0.0 copy-done
  169.2 6.3 %shard_map.86 = (bf16[4,32,4096]{2,1,0:T(8,128)(2,1)}, bf16[4,32,4096]{2,1,0:T(8,128)(2,1)}, bf16[4,32,4096]{2,1,0:T(8,128)(2,1)}) custom-call(s32[4]{0:T(128)} %copy-done, bf16[4,4,8,96,128]{4,3,2,1,0:T(8,128)(2,1)} %bitcast.10), custom_call_target="tpu_custom_call" | custom-call | tf_op jit(solution)/shard_map/pallas_call | solution.py:260
  (2 shorter events, 0.0 us)
Async XLA Ops:
  2.6 166.6 %copy-start = (s32[4]{0:T(128)}, s32[4]{0:T(128)S(1)}, u32[]{:S(2)}) copy-start(s32[4]{0:T(128)S(1)} %dynamic-slice_bitcast_fusion.mine) | copy-start | bytes 52

commit v4 on v3

--- a/solution.py
+++ b/solution.py
@@ -195,9 +195,11 @@
 def deliver(heads, page, mine, home, q_out, k_out, v_out):
     for p in range(mine.shape[0]):
         bucket = mine[p]
-        for h in range(heads):
-            for a, dst in enumerate((q_out, k_out, v_out)):
-                dst[p, :, pl.ds(h * HD, HD)] = home[h, bucket, 0, pl.ds(a * page, page), :]
+        for g in range(home.shape[2]):
+            for h in range(heads):
+                column = (g * heads + h) * HD
+                for a, dst in enumerate((q_out, k_out, v_out)):
+                    dst[p, :, pl.ds(column, HD)] = home[h, bucket, g, pl.ds(a * page, page), :]
 
 
 def shards(queries, keys, values, grad_out, page_dest, doc_start):
@@ -257,15 +259,16 @@
             flops=10 * pairs * HD, bytes_accessed=14 * tok_dev * width, transcendentals=pairs
         ),
     )(table, *(a.reshape(n_bucket, page, width) for a in (queries, keys, values, grad_out)))
+    groups = max(1, n_head // 4)
     outs = pl.pallas_call(
         functools.partial(deliver, heads, page),
-        grid=(n_head,),
+        grid=(n_head // groups,),
         out_shape=[jax.ShapeDtypeStruct((n_bucket, page, width), low)] * 3,
         in_specs=[
             smem,
-            pl.BlockSpec((heads, n_bucket, 1, back_rows, HD), lambda g: (0, 0, g, 0, 0)),
+            pl.BlockSpec((heads, n_bucket, groups, back_rows, HD), lambda g: (0, 0, g, 0, 0)),
         ],
-        out_specs=[pl.BlockSpec((n_bucket, page, heads * HD), lambda g: (0, 0, g))] * 3,
+        out_specs=[pl.BlockSpec((n_bucket, page, groups * heads * HD), lambda g: (0, 0, g))] * 3,
     )(mine, home.reshape(heads, n_bucket, n_head, back_rows, HD))
     return tuple(a.reshape(tok_dev, width) for a in outs)
 

time: 176 us -> 174 us (0.989)
  Pallas kernels: 172 us -> 170 us
    pallas_call x1, Pallas kernels: 6.33 us -> 4.41 us  [shards(): pl.pallas_call(functools.partial(deliver, heads, page), grid=(n_head // g...]
where the time goes in v4:
time: 174 us
  Pallas kernels  170 us (98%)
  local copies, waits for them, and re-layouts  1.78 us (1%)
    pallas_call x1, Pallas kernels, shards(): pl.pallas_call(functools.partial(kernel, n_bucket, n_head, heads, page, b...  166 us
    pallas_call x1, Pallas kernels, shards(): pl.pallas_call(functools.partial(deliver, heads, page), grid=(n_head // g...  4.41 us

profile of v4, /device:TPU:0, one launch (start us, length us, event | category | flops | bytes accessed | tf_op | source)
XLA Modules:
  0.0 173.6 jit_solution(17272845726256097398)
XLA Ops:
  0.6 0.7 dynamic_slice.8
  1.4 0.1 reshape.50
  1.5 0.1 slice_reduce_fusion
  1.6 0.1 compare_convert_fusion
  1.7 0.1 reshape.59
  1.7 0.8 reshape.49
  2.5 0.1 fusion.1
  2.6 0.0 copy-start
  2.7 0.1 select_reduce_fusion.1
  2.7 0.1 select_reduce_fusion
  2.8 0.6 pad_add_fusion.table
  3.4 165.8 %shard_map.85 = bf16[4,32,96,128]{3,2,1,0:T(8,128)(2,1)} custom-call(s32[84]{0:T(128)} %pad_add_fusion.table, bf16[4,32,4096]{2,1,0:T(8,128)(2,1)} %bitcast.11, bf16[4,32,4096]{2,1,0:T(8,128)(2,1)} %bitcast.12, bf16[4,32,4096]{2,1,0:T(8,128)(2,1)} %bitcast.13, bf16[4,32,4096]{2,1,0:T(8,128)(2,1)} %bitcast.14), custom_call_target="tpu_custom_call" | custom-call | flops 2684354560 | bytes 7340032 | tf_op jit(solution)/shard_map/pallas_call | solution.py:224
  169.2 0.0 copy-done
  169.2 4.4 %shard_map.86 = (bf16[4,32,4096]{2,1,0:T(8,128)(2,1)}, bf16[4,32,4096]{2,1,0:T(8,128)(2,1)}, bf16[4,32,4096]{2,1,0:T(8,128)(2,1)}) custom-call(s32[4]{0:T(128)} %copy-done, bf16[4,4,8,96,128]{4,3,2,1,0:T(8,128)(2,1)} %bitcast.10), custom_call_target="tpu_custom_call" | custom-call | tf_op jit(solution)/shard_map/pallas_call | solution.py:263
  (2 shorter events, 0.0 us)
Async XLA Ops:
  2.6 166.6 %copy-start = (s32[4]{0:T(128)}, s32[4]{0:T(128)S(1)}, u32[]{:S(2)}) copy-start(s32[4]{0:T(128)S(1)} %dynamic-slice_bitcast_fusion.mine) | copy-start | bytes 52

commit v5 on v4

--- a/solution.py
+++ b/solution.py
@@ -79,6 +79,14 @@
             barrier, inc=1, device_id=(d // n_head, lax.rem(d, n_head)), device_id_type=MESH
         )
 
+    halves = 2 if n_head % 2 == 0 else 1
+
+    def target(step):
+        pair = step // halves
+        ahead = lax.rem(step, halves) * (n_head // halves) + pair // n_bucket
+        b = lax.rem(lax.axis_index("bucket") + lax.rem(pair, n_bucket), n_bucket)
+        return b * n_head + lax.rem(lax.axis_index("head") + ahead, n_head)
+
     def pack(h, d, where):
         from_page = table[d // n_head]
         column = pl.multiple_of((lax.rem(d, n_head) * heads + h) * HD, HD)
@@ -93,7 +101,7 @@
     def _(h):
         @pl.loop(1, n)
         def _(step):
-            d = lax.rem(me + step, n)
+            d = target(step)
             pack(h, d, send)
             pltpu.make_async_remote_copy(
                 src_ref=send.at[h, d],
@@ -170,7 +178,7 @@
 
         @pl.loop(1, n)
         def _(step):
-            d = lax.rem(me + step, n)
+            d = target(step)
             pack_back(h, d)
             pltpu.make_async_remote_copy(
                 src_ref=back.at[h, d],

time: 174 us -> 175 us (level)
  Pallas kernels: 170 us -> 172 us
where the time goes in v5:
time: 175 us
  Pallas kernels  172 us (98%)
  local copies, waits for them, and re-layouts  1.78 us (1%)
    pallas_call x1, Pallas kernels, shards(): pl.pallas_call(functools.partial(kernel, n_bucket, n_head, heads, page, b...  167 us
    pallas_call x1, Pallas kernels, shards(): pl.pallas_call(functools.partial(deliver, heads, page), grid=(n_head // g...  4.41 us

profile of v5, /device:TPU:0, one launch (start us, length us, event | category | flops | bytes accessed | tf_op | source)
XLA Modules:
  0.0 175.1 jit_solution(1814949682653141078)
XLA Ops:
  0.6 0.7 dynamic_slice.8
  1.4 0.1 reshape.50
  1.5 0.1 slice_reduce_fusion
  1.6 0.1 compare_convert_fusion
  1.7 0.1 reshape.59
  1.7 0.8 reshape.49
  2.5 0.1 fusion.1
  2.6 0.0 copy-start
  2.7 0.1 select_reduce_fusion.1
  2.7 0.1 select_reduce_fusion
  2.8 0.6 pad_add_fusion.table
  3.4 167.2 %shard_map.85 = bf16[4,32,96,128]{3,2,1,0:T(8,128)(2,1)} custom-call(s32[84]{0:T(128)} %pad_add_fusion.table, bf16[4,32,4096]{2,1,0:T(8,128)(2,1)} %bitcast.11, bf16[4,32,4096]{2,1,0:T(8,128)(2,1)} %bitcast.12, bf16[4,32,4096]{2,1,0:T(8,128)(2,1)} %bitcast.13, bf16[4,32,4096]{2,1,0:T(8,128)(2,1)} %bitcast.14), custom_call_target="tpu_custom_call" | custom-call | flops 2684354560 | bytes 7340032 | tf_op jit(solution)/shard_map/pallas_call | solution.py:232
  170.7 0.0 copy-done
  170.7 4.4 %shard_map.86 = (bf16[4,32,4096]{2,1,0:T(8,128)(2,1)}, bf16[4,32,4096]{2,1,0:T(8,128)(2,1)}, bf16[4,32,4096]{2,1,0:T(8,128)(2,1)}) custom-call(s32[4]{0:T(128)} %copy-done, bf16[4,4,8,96,128]{4,3,2,1,0:T(8,128)(2,1)} %bitcast.10), custom_call_target="tpu_custom_call" | custom-call | tf_op jit(solution)/shard_map/pallas_call | solution.py:271
  (2 shorter events, 0.0 us)
Async XLA Ops:
  2.6 168.0 %copy-start = (s32[4]{0:T(128)}, s32[4]{0:T(128)S(1)}, u32[]{:S(2)}) copy-start(s32[4]{0:T(128)S(1)} %dynamic-slice_bitcast_fusion.mine) | copy-start | bytes 52
